TPU v7x, 512 devices: a whole 4x4x16 slice. The times are simulated.
512 devices in a mesh: grp: 16 (over x, y), dev: 32 (over z, core).
Axes of the slice: x: 4, y: 4, z: 16, core: 2. Of those that a mesh axis runs over, the one named last changes fastest.
Arguments:
- block_vectors: float32 [262144, 64], P(('grp', 'dev')), may hold values from -6 to 6
- hamiltonian: float32 [4096, 64, 2048], P(('grp', 'dev')), may hold values from -0.125 to 0.125
- pattern: int32 [4096, 32], P(('grp', 'dev')), may hold values from 0 to 4095, as said below
- owned_blocks: int32 [512], P(('grp', 'dev')), may hold values from 1 to 8, as said below
- spectrum: float32 [2], replicated, may hold values from 0.5 to 2
Outputs:
- basis: float32 [262144, 64], P(('grp', 'dev'))
- r_factor: float32 [64, 64], replicated
Inputs may be any that keep to these rules, and one draw needn't show every extreme that they name: pattern[b, 0] = b; every other entry is b + o clipped to the slots, for a distinct nonzero o with |o| <= 16. `owned_blocks`: some device owns all 8 slots.
All inputs are finite; a program needn't handle non-finite values.
Results may differ from a plain program's by a relative error of at most 0.0003.
Values sent between devices are 32-bit elements; how exact they have to be, the bound alone decides.
A program may use at most 64 MiB of HBM per device.

v0:
```python
import jax
import jax.numpy as jnp
from jax import lax
from jax.sharding import PartitionSpec as P

BAND = 16


def shifted(block, axis, distance):
    devices = range(lax.axis_size(axis))
    route = [(i - distance, i) for i in devices if i - distance in devices]
    return lax.ppermute(block, axis, route)


def send_direct(values, distance):
    return shifted(values, ("grp", "dev"), distance)


def extend_band(values, reach_dev):
    lowers = []
    uppers = []
    for distance in range(reach_dev, 0, -1):
        lowers.append(send_direct(values, distance))
    for distance in range(1, reach_dev + 1):
        uppers.append(send_direct(values, -distance))
    return jnp.concatenate(lowers + [values] + uppers, axis=0)


def apply_matrix(values, hamiltonian, local_index, reach_dev):
    extended = extend_band(values, reach_dev)
    block_count, neighbours = local_index.shape
    picked = jnp.take(extended, local_index, axis=0)
    picked = picked.reshape(block_count, neighbours * values.shape[1], values.shape[2])
    return jnp.einsum("gik,gkc->gic", hamiltonian, picked, precision=lax.Precision.HIGHEST)


def summed_gram(flat):
    local_gram = jnp.dot(
        flat.T, flat, precision=lax.Precision.HIGHEST, preferred_element_type=jnp.float32
    )
    return lax.psum(local_gram, ("grp", "dev"))


def cholesky_step(flat):
    gram_total = summed_gram(flat)
    upper = jnp.linalg.cholesky(gram_total).T
    ortho = jax.scipy.linalg.solve_triangular(upper.T, flat.T, lower=True).T
    return (ortho, upper)


def on_device(block_vectors, hamiltonian, pattern, owned_blocks, spectrum):
    block_count = pattern.shape[0]
    block_size = hamiltonian.shape[1]
    columns = block_vectors.shape[1]
    reach_dev = (BAND + block_count - 1) // block_count
    first_block = lax.axis_index(("grp", "dev")) * block_count
    local_index = pattern - first_block + reach_dev * block_count
    live_mask = (jnp.arange(block_count, dtype=jnp.int32) < owned_blocks[0]).astype(jnp.float32)[
        :, None, None
    ]
    shift_value = spectrum[0]
    scale_value = spectrum[1]
    first_vec = block_vectors.reshape(block_count, block_size, columns) * live_mask
    second_vec = live_mask * (
        (apply_matrix(first_vec, hamiltonian, local_index, reach_dev) - shift_value * first_vec)
        / scale_value
    )
    third_vec = live_mask * (
        2.0
        * (apply_matrix(second_vec, hamiltonian, local_index, reach_dev) - shift_value * second_vec)
        / scale_value
        - first_vec
    )
    flat = third_vec.reshape(block_count * block_size, columns)
    ortho_one, upper_one = cholesky_step(flat)
    ortho_two, upper_two = cholesky_step(ortho_one)
    upper_all = jnp.dot(
        upper_two, upper_one, precision=lax.Precision.HIGHEST, preferred_element_type=jnp.float32
    )
    total = jnp.sqrt(
        jnp.float32(block_count * block_size * lax.axis_size("grp") * lax.axis_size("dev"))
    )
    return (ortho_two * total, upper_all / total)


def solution(mesh):
    placed = (
        P(("grp", "dev"), None),
        P(("grp", "dev"), None, None),
        P(("grp", "dev"), None),
        P(("grp", "dev")),
        P(),
    )
    return jax.shard_map(
        on_device,
        mesh=mesh,
        in_specs=placed,
        out_specs=(P(("grp", "dev"), None), P()),
        check_vma=False,
    )
```

profile of v0, /device:TPU:1, one launch (start us, length us, event | category | flops | bytes accessed | tf_op | source)
XLA Modules:
  0.0 355.4 jit_solution(15956783039810358615)
XLA Ops:
  1.3 1.0 reshape.34
  2.4 1.3 collective-permute-start.3
  3.7 8.8 %collective-permute-start.2 = (f32[8,64,64]{1,2,0:T(8,128)S(1)}, f32[8,64,64]{1,2,0:T(8,128)S(1)}, u32[]{:S(2)}, u32[]{:S(2)}) collective-permute-start(f32[8,64,64]{1,2,0:T(8,128)S(1)} %copy_multiply_fusion), channel_id=1, source_target_pairs={{1,0},{2,1},{3,2},{4,3},{5,4},{6,5},{7,6},{8,7},{9,8},{10,9},{11,1... | collective-permute-start | bytes 393224 | tf_op jit(solution)/shard_map/ppermute | solution.py:12
  12.5 4.2 %collective-permute-start.1 = (f32[8,64,64]{1,2,0:T(8,128)S(1)}, f32[8,64,64]{1,2,0:T(8,128)S(1)}, u32[]{:S(2)}, u32[]{:S(2)}) collective-permute-start(f32[8,64,64]{1,2,0:T(8,128)S(1)} %copy_multiply_fusion), channel_id=1, source_target_pairs={{0,1},{1,2},{2,3},{3,4},{4,5},{5,6},{6,7},{7,8},{8,9},{9,10},{10,1... | collective-permute-start | bytes 393224 | tf_op jit(solution)/shard_map/ppermute | solution.py:12
  16.7 2.0 collective-permute-start
  19.4 1.3 fusion.29
  20.8 4.5 %collective-permute-done = f32[8,64,64]{1,2,0:T(8,128)S(1)} collective-permute-done((f32[8,64,64]{1,2,0:T(8,128)S(1)}, f32[8,64,64]{1,2,0:T(8,128)S(1)}, u32[]{:S(2)}, u32[]{:S(2)}) %collective-permute-start) | collective-permute-done | bytes 131104 | tf_op jit(solution)/shard_map/ppermute | solution.py:12
  25.6 4.4 %gather_fusion = f32[256,64,64]{1,2,0:T(8,128)} fusion(f32[40,64,64]{1,2,0:T(8,128)S(1)} %constant_dynamic-update-slice_fusion, s32[1024]{0:T(1024)S(1)} %pad_clamp_fusion), kind=kCustom, calls=%fused_computation.clone | custom fusion | bytes 8389632 | tf_op jit(solution)/shard_map/jit(_take)/gather | solution.py:32
  29.9 3.8 %broadcast_select_fusion.1 = f32[8,32,64,64]{2,3,1,0:T(8,128)S(1)} fusion(f32[8,32,64,64]{2,3,1,0:T(8,128)} %bitcast.73, pred[8,32]{1,0:T(8,128)(4,1)S(1)} %get-tuple-element.4), kind=kLoop, calls=%fused_computation.3 | loop fusion | flops 1048576 | bytes 8388864 | tf_op jit(solution)/shard_map/jit(_take)/select_n | solution.py:32
  33.8 8.0 %copy.15 = f32[8,32,64,64]{2,1,3,0:T(8,128)} copy(f32[8,32,64,64]{2,3,1,0:T(8,128)S(1)} %broadcast_select_fusion.1) | data formatting | bytes 8388608 | tf_op jit(solution)/shard_map/jit(_take)/select_n | solution.py:32
  41.8 7.8 %reshape.35 = f32[8,2048,64]{1,2,0:T(8,128)} reshape(f32[8,32,64,64]{2,1,3,0:T(8,128)} %copy.15) | data formatting | bytes 8388608 | tf_op jit(solution)/shard_map/reshape | solution.py:33
  49.6 8.7 %fusion.4 = f32[8,64,64]{1,2,0:T(8,128)S(1)} fusion(f32[8,2048,64]{1,2,0:T(8,128)} %reshape.35, f32[8,64,2048]{2,1,0:T(8,128)} %param.11, f32[]{:T(128)} %bitcast.4, f32[]{:T(128)} %bitcast.3, f32[8]{0:T(128)S(1)} %compare_convert_fusion, f32[8,64,64]{1,0,2:T(8,128)S(1)} %reshape.34), kind=kOutput, calls=%fused_computation.10 | convolution fusion | flops 805470208 | bytes 8650792 | tf_op jit(solution)/shard_map/gik,gkc->gic/dot_general | solution.py:34
  58.3 4.1 %collective-permute-start.4 = (f32[8,64,64]{1,2,0:T(8,128)S(1)}, f32[8,64,64]{1,2,0:T(8,128)S(1)}, u32[]{:S(2)}, u32[]{:S(2)}) collective-permute-start(f32[8,64,64]{1,2,0:T(8,128)S(1)} %fusion.4), channel_id=1, source_target_pairs={{0,2},{1,3},{2,4},{3,5},{4,6},{5,7},{6,8},{7,9},{8,10},{9,11},{10,... | collective-permute-start | bytes 393224 | tf_op jit(solution)/shard_map/ppermute | solution.py:12
  62.4 2.7 collective-permute-start.5
  65.1 1.3 collective-permute-start.7
  66.4 2.1 collective-permute-start.6
  68.5 2.8 collective-permute-done.5
  71.3 6.5 %collective-permute-done.6 = f32[8,64,64]{1,2,0:T(8,128)S(1)} collective-permute-done((f32[8,64,64]{1,2,0:T(8,128)S(1)}, f32[8,64,64]{1,2,0:T(8,128)S(1)}, u32[]{:S(2)}, u32[]{:S(2)}) %collective-permute-start.6) | collective-permute-done | bytes 131104 | tf_op jit(solution)/shard_map/ppermute | solution.py:12
  77.9 4.4 %gather_fusion.1 = f32[256,64,64]{1,2,0:T(8,128)} fusion(f32[40,64,64]{1,2,0:T(8,128)S(1)} %constant_dynamic-update-slice_fusion.5, s32[1024]{0:T(1024)S(1)} %pad_clamp_fusion), kind=kCustom, calls=%fused_computation.1.clone | custom fusion | bytes 8389632 | tf_op jit(solution)/shard_map/jit(_take)/gather | solution.py:32
  82.2 3.8 %broadcast_select_fusion = f32[8,32,64,64]{2,3,1,0:T(8,128)S(1)} fusion(f32[8,32,64,64]{2,3,1,0:T(8,128)} %bitcast.72, pred[8,32]{1,0:T(8,128)(4,1)S(1)} %get-tuple-element.4), kind=kLoop, calls=%fused_computation.2 | loop fusion | flops 1048576 | bytes 8388864 | tf_op jit(solution)/shard_map/jit(_take)/select_n | solution.py:32
  86.1 8.0 %copy.16 = f32[8,32,64,64]{2,1,3,0:T(8,128)} copy(f32[8,32,64,64]{2,3,1,0:T(8,128)S(1)} %broadcast_select_fusion) | data formatting | bytes 8388608 | tf_op jit(solution)/shard_map/jit(_take)/select_n | solution.py:32
  94.1 7.8 %reshape.36 = f32[8,2048,64]{1,2,0:T(8,128)} reshape(f32[8,32,64,64]{2,1,3,0:T(8,128)} %copy.16) | data formatting | bytes 8388608 | tf_op jit(solution)/shard_map/reshape | solution.py:33
  101.9 8.7 %fusion.7 = f32[8,64,64]{1,2,0:T(8,128)S(1)} fusion(f32[8,2048,64]{1,2,0:T(8,128)} %reshape.36, f32[8,64,2048]{2,1,0:T(8,128)} %param.11, f32[8,64,64]{1,2,0:T(8,128)S(1)} %fusion.4, f32[]{:T(128)} %bitcast.4, f32[]{:T(128)} %bitcast.3, f32[8]{0:T(128)S(1)} %compare_convert_fusion, f32[8,64,64]{1,0,2:T(8,128)S(1)} %reshape.34), kind=kOutput, calls=%fused_computation.13 | convolution fusion | flops 805535744 | bytes 8781864 | tf_op jit(solution)/shard_map/gik,gkc->gic/dot_general | solution.py:34
  111.1 116.5 %psum.14 = f32[64,64]{0,1:T(8,128)S(1)} all-reduce(f32[64,64]{0,1:T(8,128)S(1)} %convolution_bitcast_fusion.2), channel_id=1, replica_groups=mesh['grp'=16,'dev'=32] {'grp','dev'}, use_global_device_ids=true, to_apply=%region_0.0 | all-reduce | flops 4096 | bytes 32768 | tf_op jit(solution)/shard_map/psum | solution.py:41
  227.9 5.8 %cholesky.44 = f32[64,64]{1,0:T(8,128)S(1)} custom-call(f32[64,64]{1,0:T(8,128)S(1)} %fusion.14), custom_call_target="Cholesky" | custom-call | tf_op jit(solution)/shard_map/jit(cholesky)/cholesky | solution.py:46
  235.1 4.9 %custom-call.6 = f32[1,64,64]{1,2,0:T(8,128)S(1)} custom-call(f32[1,64,64]{2,1,0:T(8,128)S(1)} %fusion.18), custom_call_target="InvertDiagBlocksLowerTriangular" | custom-call | tf_op jit(solution)/shard_map/jit(_solve_triangular)/triangular_solve | solution.py:47
  240.6 99.3 %psum.15 = f32[64,64]{0,1:T(8,128)S(1)} all-reduce(f32[64,64]{0,1:T(8,128)S(1)} %fusion.30), channel_id=1, replica_groups=mesh['grp'=16,'dev'=32] {'grp','dev'}, use_global_device_ids=true, to_apply=%region_3.7 | all-reduce | flops 4096 | bytes 32768 | tf_op jit(solution)/shard_map/psum | solution.py:41
  340.0 5.8 %cholesky.55 = f32[64,64]{1,0:T(8,128)S(1)} custom-call(f32[64,64]{1,0:T(8,128)S(1)} %fusion.12), custom_call_target="Cholesky" | custom-call | tf_op jit(solution)/shard_map/jit(cholesky)/cholesky | solution.py:46
  345.9 0.7 compare_reduce_fusion
  346.6 2.2 convolution_multiply_fusion.1
  349.5 4.9 %custom-call.7 = f32[1,64,64]{1,2,0:T(8,128)S(1)} custom-call(f32[1,64,64]{2,1,0:T(8,128)S(1)} %select_bitcast_fusion), custom_call_target="InvertDiagBlocksLowerTriangular" | custom-call | tf_op jit(solution)/shard_map/jit(_solve_triangular)/triangular_solve | solution.py:47
  354.4 1.0 fusion.8
  (34 shorter events, 4.6 us)
Async XLA Ops:
  2.4 23.1 %collective-permute-start.3 = (f32[8,64,64]{1,2,0:T(8,128)S(1)}, f32[8,64,64]{1,2,0:T(8,128)S(1)}, u32[]{:S(2)}, u32[]{:S(2)}) collective-permute-start(f32[8,64,64]{1,2,0:T(8,128)S(1)} %copy_multiply_fusion), channel_id=1, source_target_pairs={{2,0},{3,1},{4,2},{5,3},{6,4},{7,5},{8,6},{9,7},{10,8},{11,9},{12,... | collective-permute-start | bytes 393224 | tf_op jit(solution)/shard_map/ppermute | solution.py:12
  3.7 21.8 %collective-permute-start.2 = (f32[8,64,64]{1,2,0:T(8,128)S(1)}, f32[8,64,64]{1,2,0:T(8,128)S(1)}, u32[]{:S(2)}, u32[]{:S(2)}) collective-permute-start(f32[8,64,64]{1,2,0:T(8,128)S(1)} %copy_multiply_fusion), channel_id=1, source_target_pairs={{1,0},{2,1},{3,2},{4,3},{5,4},{6,5},{7,6},{8,7},{9,8},{10,9},{11,1... | collective-permute-start | bytes 393224 | tf_op jit(solution)/shard_map/ppermute | solution.py:12
  12.5 12.9 %collective-permute-start.1 = (f32[8,64,64]{1,2,0:T(8,128)S(1)}, f32[8,64,64]{1,2,0:T(8,128)S(1)}, u32[]{:S(2)}, u32[]{:S(2)}) collective-permute-start(f32[8,64,64]{1,2,0:T(8,128)S(1)} %copy_multiply_fusion), channel_id=1, source_target_pairs={{0,1},{1,2},{2,3},{3,4},{4,5},{5,6},{6,7},{7,8},{8,9},{9,10},{10,1... | collective-permute-start | bytes 393224 | tf_op jit(solution)/shard_map/ppermute | solution.py:12
  16.7 8.7 %collective-permute-start = (f32[8,64,64]{1,2,0:T(8,128)S(1)}, f32[8,64,64]{1,2,0:T(8,128)S(1)}, u32[]{:S(2)}, u32[]{:S(2)}) collective-permute-start(f32[8,64,64]{1,2,0:T(8,128)S(1)} %copy_multiply_fusion), channel_id=1, source_target_pairs={{0,2},{1,3},{2,4},{3,5},{4,6},{5,7},{6,8},{7,9},{8,10},{9,11},{10,... | collective-permute-start | bytes 393224 | tf_op jit(solution)/shard_map/ppermute | solution.py:12
  58.3 10.2 %collective-permute-start.4 = (f32[8,64,64]{1,2,0:T(8,128)S(1)}, f32[8,64,64]{1,2,0:T(8,128)S(1)}, u32[]{:S(2)}, u32[]{:S(2)}) collective-permute-start(f32[8,64,64]{1,2,0:T(8,128)S(1)} %fusion.4), channel_id=1, source_target_pairs={{0,2},{1,3},{2,4},{3,5},{4,6},{5,7},{6,8},{7,9},{8,10},{9,11},{10,... | collective-permute-start | bytes 393224 | tf_op jit(solution)/shard_map/ppermute | solution.py:12
  62.4 8.9 %collective-permute-start.5 = (f32[8,64,64]{1,2,0:T(8,128)S(1)}, f32[8,64,64]{1,2,0:T(8,128)S(1)}, u32[]{:S(2)}, u32[]{:S(2)}) collective-permute-start(f32[8,64,64]{1,2,0:T(8,128)S(1)} %fusion.4), channel_id=1, source_target_pairs={{0,1},{1,2},{2,3},{3,4},{4,5},{5,6},{6,7},{7,8},{8,9},{9,10},{10,1... | collective-permute-start | bytes 393224 | tf_op jit(solution)/shard_map/ppermute | solution.py:12
  65.1 12.8 %collective-permute-start.7 = (f32[8,64,64]{1,2,0:T(8,128)S(1)}, f32[8,64,64]{1,2,0:T(8,128)S(1)}, u32[]{:S(2)}, u32[]{:S(2)}) collective-permute-start(f32[8,64,64]{1,2,0:T(8,128)S(1)} %fusion.4), channel_id=1, source_target_pairs={{2,0},{3,1},{4,2},{5,3},{6,4},{7,5},{8,6},{9,7},{10,8},{11,9},{12,... | collective-permute-start | bytes 393224 | tf_op jit(solution)/shard_map/ppermute | solution.py:12
  66.4 11.4 %collective-permute-start.6 = (f32[8,64,64]{1,2,0:T(8,128)S(1)}, f32[8,64,64]{1,2,0:T(8,128)S(1)}, u32[]{:S(2)}, u32[]{:S(2)}) collective-permute-start(f32[8,64,64]{1,2,0:T(8,128)S(1)} %fusion.4), channel_id=1, source_target_pairs={{1,0},{2,1},{3,2},{4,3},{5,4},{6,5},{7,6},{8,7},{9,8},{10,9},{11,1... | collective-permute-start | bytes 393224 | tf_op jit(solution)/shard_map/ppermute | solution.py:12
where the time goes:
time: 356 us; the launch traced here: 355 us
  blocking collectives  216 us (61%)
  local copies, waits for them, and re-layouts  43.3 us (12%)
  other arithmetic  32.9 us (9%)
  starting transfers between devices  26.5 us (7%)
  matrix products  21.5 us (6%)
  waiting for transfers between devices  13.8 us (4%)
    psum x2, blocking collectives, summed_gram(): return lax.psum(local_gram, ('grp', 'dev'))  216 us
    ppermute x8, starting transfers between devices, shifted(): return lax.ppermute(block, axis, route)  26.5 us
    dot_general x2, matrix products, apply_matrix(): jnp.einsum('gik,gkc->gic', hamiltonian, picked, precision=lax.Precision.H...  17.4 us
    select_n x2, local copies, waits for them, and re-layouts, apply_matrix(): picked = jnp.take(extended, local_index, axis=0)  16 us
    reshape x2, local copies, waits for them, and re-layouts, apply_matrix(): picked.reshape(block_count, neighbours * values.shape[1], values.shape[2])  15.6 us
    ppermute x8, waiting for transfers between devices, shifted(): return lax.ppermute(block, axis, route)  13.8 us
    another operation x6, other arithmetic, cholesky_step(): upper = jnp.linalg.cholesky(gram_total).T  13.1 us
    another operation x4, other arithmetic, cholesky_step(): ortho = jax.scipy.linalg.solve_triangular(upper.T, flat.T, lower=True).T  11.1 us
  transfers between devices with their start and end apart: 8, of which 3 were waited for; matrix products, arithmetic and copies ran while one was open for 1% of the time, Pallas kernels for 0%

commit v1 on v0

v1 whole, which is shorter than its diff:
```python
import functools

import jax
import jax.numpy as jnp
from jax import lax
from jax.experimental import pallas as pl
from jax.experimental.pallas import tpu as pltpu
from jax.sharding import PartitionSpec as P

BAND = 16
MESH = pl.DeviceIdType.MESH
HIGHEST = lax.Precision.HIGHEST
LANES = 128


def low_lanes(shape):
    return lax.broadcasted_iota(jnp.int32, shape, len(shape) - 1) < shape[-1] // 2


def swap_halves(value):
    return pltpu.roll(value, value.shape[-1] // 2, value.ndim - 1)


def filter_kernel(
    groups, members, blocks, size, neighbours, reach,
    xt_ref, ham_ref, pat_ref, owned_ref, spec_ref,
    y_out, g_out,
    y_buf, xt_buf, h_buf, h_split, v_split, ext_one, ext_two,
    part_buf, scatter_buf, own_buf, reduce_buf, sum_buf, total_buf,
    xt_sem, h_sem, send_one, recv_one, send_two, recv_two, red_sem, round_sem, y_sem,
):
    grp = lax.axis_index("grp")
    dev = lax.axis_index("dev")
    flat = grp * members + dev
    devices = groups * members
    half = blocks // 2
    distances = [d for d in range(-reach, reach + 1) if d]

    def peer(distance):
        other = lax.rem(flat + distance + devices, devices)
        return (lax.div(other, members), lax.rem(other, members))

    def in_groups(step):
        return (lax.rem(grp + step, groups), dev)

    def in_members(step):
        return (grp, lax.rem(dev + step, members))

    x_copy = pltpu.make_async_copy(xt_ref, xt_buf, xt_sem)
    x_copy.start()

    def h_copy(b):
        return pltpu.make_async_copy(ham_ref.at[b], h_buf.at[b], h_sem.at[b])

    for b in range(blocks):
        h_copy(b).start()

    def distinct(offsets, count):
        return sorted({offset % count for offset in offsets} - {0})

    def greet(sem, targets):
        for target in targets:
            pl.semaphore_signal(sem, inc=1, device_id=target, device_id_type=MESH)
        return len(targets)

    def group_ring(offsets):
        return [in_groups(step) for step in distinct(offsets, groups)]

    def member_ring(offsets):
        return [in_members(step) for step in distinct(offsets, members)]

    other_core = dev + 1 - 2 * lax.rem(dev, 2)
    siblings = [
        (grp, lax.rem(other_core + step, members)) for step in [0] + distinct((2, -2), members)
    ]
    barrier = pltpu.get_barrier_semaphore()
    greeted = greet(
        barrier,
        [peer(distance) for distance in distances]
        + siblings
        + member_ring((2, -2))
        + group_ring((1, -1, 4, -4)),
    )
    rounds = [
        member_ring((2, -2)) + group_ring((1, -1, 4, -4)),
        member_ring((4, -4)) + group_ring((4, -4)),
        member_ring((8, -8)),
    ]

    def greet_round(k):
        greet(round_sem.at[k], rounds[k])

    def end_round(k):
        if rounds[k]:
            pl.semaphore_wait(round_sem.at[k], len(rounds[k]))

    owned = owned_ref[0]
    shift = spec_ref[0]
    scale = spec_ref[1]
    low = low_lanes((size, LANES))

    def live(p):
        first = jnp.where(p < owned, 1.0, 0.0).astype(jnp.float32)
        second = jnp.where(p + half < owned, 1.0, 0.0).astype(jnp.float32)
        return jnp.where(low, first, second)

    x_copy.wait()
    for p in range(half):
        both = jnp.concatenate(
            [
                xt_buf[:, p * size : (p + 1) * size],
                xt_buf[:, (p + half) * size : (p + half + 1) * size],
            ],
            axis=0,
        )
        ext_one[reach, p] = live(p) * both.T

    def halo_one(k):
        distance = distances[k]
        return pltpu.make_async_remote_copy(
            src_ref=ext_one.at[reach],
            dst_ref=ext_one.at[reach - distance],
            send_sem=send_one.at[k],
            recv_sem=recv_one.at[k],
            device_id=peer(distance),
            device_id_type=MESH,
        )

    def halo_two(k, p):
        distance = distances[k]
        return pltpu.make_async_remote_copy(
            src_ref=ext_two.at[reach, p],
            dst_ref=ext_two.at[reach - distance, p],
            send_sem=send_two.at[k, p],
            recv_sem=recv_two.at[k, p],
            device_id=peer(distance),
            device_id_type=MESH,
        )

    pl.semaphore_wait(barrier, greeted)
    for k in range(len(distances)):
        halo_one(k).start()
    greet_round(0)

    rows = 16

    @pl.loop(0, blocks)
    def _(b):
        h_copy(b).wait()
        for r in range(0, size, rows):
            value = h_buf[b, r : r + rows, :]
            high = value.astype(jnp.bfloat16)
            h_split[b, r : r + rows, :] = high
            h_split[b, size + r : size + r + rows, :] = (
                value - high.astype(jnp.float32)
            ).astype(jnp.bfloat16)

    def split(ext, slot):
        for p in range(half):
            value = ext[slot, p]
            high = value.astype(jnp.bfloat16).astype(jnp.float32)
            rest = value - high
            v_split[slot * blocks + p] = jnp.where(low, high, swap_halves(rest)).astype(
                jnp.bfloat16
            )
            v_split[slot * blocks + p + half] = jnp.where(
                low, swap_halves(high), rest
            ).astype(jnp.bfloat16)

    start = flat * blocks - reach * blocks
    depth = 4
    last = (2 * reach + 1) * blocks - 1

    def place(b, k):
        return jnp.clip(pat_ref[b, k] - start, 0, last)

    def product(b):
        total = jnp.zeros((2 * size, LANES), jnp.float32)
        for t in range(0, neighbours, depth):
            picked = jnp.concatenate(
                [v_split[place(b, t + q)] for q in range(depth)], axis=0
            )
            total += jnp.dot(
                h_split[b, :, t * size : (t + depth) * size],
                picked,
                preferred_element_type=jnp.float32,
            )
        both = total[:size] + total[size:]
        return both + swap_halves(both)

    def apply_matrix(p):
        return jnp.where(low, product(p), product(p + half))

    split(ext_one, reach)
    for k in range(len(distances)):
        halo_one(k).wait()
        split(ext_one, reach - distances[k])
    end_round(0)
    greet_round(1)

    @pl.loop(0, half)
    def _(p):
        first = ext_one[reach, p]
        ext_two[reach, p] = live(p) * ((apply_matrix(p) - shift * first) / scale)
        for k in range(len(distances)):
            halo_two(k, p).start()

    end_round(1)
    greet_round(2)
    split(ext_two, reach)
    for k in range(len(distances)):
        for p in range(half):
            halo_two(k, p).wait()
        split(ext_two, reach - distances[k])

    @pl.loop(0, half)
    def _(p):
        second = ext_two[reach, p]
        y_buf[p] = live(p) * (
            2.0 * (apply_matrix(p) - shift * second) / scale - ext_one[reach, p]
        )

    y_copy = pltpu.make_async_copy(y_buf, y_out, y_sem)
    y_copy.start()
    gram = jnp.zeros((LANES, LANES), jnp.float32)
    for p in range(half):
        value = y_buf[p]
        gram += lax.dot_general(
            value, value, (((0,), (0,)), ((), ())),
            precision=HIGHEST, preferred_element_type=jnp.float32,
        )
    gram = gram[:size] + swap_halves(gram[size:])
    packed = jnp.where(
        low_lanes((size // 2, LANES)), gram[: size // 2], swap_halves(gram[size // 2 :])
    )
    piece = size // 2 // groups
    for m in range(groups):
        part_buf[m] = packed[m * piece : (m + 1) * piece]
    end_round(2)

    def exchange(step, who, source, target, k):
        return pltpu.make_async_remote_copy(
            src_ref=source, dst_ref=target, send_sem=red_sem.at[2 * k],
            recv_sem=red_sem.at[2 * k + 1], device_id=who(step), device_id_type=MESH,
        )

    def finish(buf, count, k):
        for sem in (2 * k, 2 * k + 1):
            pltpu.make_async_copy(
                buf.at[pl.ds(0, count)], buf.at[pl.ds(0, count)], red_sem.at[sem]
            ).wait()

    @pl.loop(1, groups)
    def _(step):
        to = lax.rem(grp + step, groups)
        exchange(step, in_groups, part_buf.at[to], scatter_buf.at[grp], 0).start()

    scatter_buf[grp] = part_buf[grp]
    finish(scatter_buf, groups - 1, 0)
    own_buf[...] = jnp.sum(scatter_buf[...], axis=0)

    @pl.loop(1, members)
    def _(step):
        exchange(step, in_members, own_buf, reduce_buf.at[dev], 1).start()

    reduce_buf[dev] = own_buf[...]
    finish(reduce_buf, members - 1, 1)
    sum_buf[...] = jnp.sum(reduce_buf[...], axis=0)

    @pl.loop(1, groups)
    def _(step):
        exchange(step, in_groups, sum_buf, total_buf.at[grp], 2).start()

    total_buf[grp] = sum_buf[...]
    finish(total_buf, groups - 1, 2)
    for m in range(groups):
        g_out[m * piece : (m + 1) * piece, :] = total_buf[m]
    y_copy.wait()


def factor_kernel(total, g_ref, y_ref, q_out, r_out, y_buf, y_sem):
    half, size, lanes = y_ref.shape
    y_copy = pltpu.make_async_copy(y_ref, y_buf, y_sem)
    y_copy.start()
    packed = g_ref[...]
    work = jnp.concatenate([packed, swap_halves(packed)], axis=0)
    row = lax.broadcasted_iota(jnp.int32, (size, lanes), 0)
    col = lax.broadcasted_iota(jnp.int32, (size, lanes), 1)
    work = jnp.where(col < size, work, jnp.where(col - size == row, 1.0, 0.0))
    for j in range(size - 1):
        lead = work[j : j + 1, :]
        lead = lead * (1.0 / lead[:, j : j + 1])
        factor = jnp.where(row > j, jnp.broadcast_to(work[:, j : j + 1], work.shape), 0.0)
        work = work - factor * lead
    diagonal = jnp.sum(jnp.where(row == col, work, 0.0), axis=1, keepdims=True)
    work = work * (1.0 / jnp.sqrt(diagonal))
    r_out[...] = jnp.where(col >= row, work, 0.0)[:, :size] * (1.0 / total)
    low = col < size
    inverse = jnp.concatenate(
        [jnp.where(low, swap_halves(work), 0.0), jnp.where(low, 0.0, work)], axis=0
    )
    inverse = inverse * total
    y_copy.wait()
    for p in range(half):
        ortho = lax.dot_general(
            inverse, y_buf[p], (((1,), (1,)), ((), ())),
            precision=HIGHEST, preferred_element_type=jnp.float32,
        )
        q_out[:, p * size : (p + 1) * size] = ortho[:size]
        q_out[:, (p + half) * size : (p + half + 1) * size] = ortho[size:]


def on_device(block_vectors, hamiltonian, pattern, owned_blocks, spectrum):
    blocks, neighbours = pattern.shape
    size = hamiltonian.shape[1]
    columns = block_vectors.shape[1]
    groups = lax.axis_size("grp")
    members = lax.axis_size("dev")
    reach = (BAND + blocks - 1) // blocks
    half = blocks // 2
    slots = 2 * reach + 1
    piece = size // 2 // groups
    f32 = jnp.float32
    vmem = pl.BlockSpec(memory_space=pltpu.VMEM)
    smem = pl.BlockSpec(memory_space=pltpu.SMEM)
    hbm = pl.BlockSpec(memory_space=pltpu.HBM)
    dma = pltpu.SemaphoreType.DMA
    filtered, gram = pl.pallas_call(
        functools.partial(filter_kernel, groups, members, blocks, size, neighbours, reach),
        out_shape=(
            jax.ShapeDtypeStruct((half, size, 2 * columns), f32),
            jax.ShapeDtypeStruct((size // 2, 2 * columns), f32),
        ),
        in_specs=[hbm, hbm, smem, smem, smem],
        out_specs=(hbm, vmem),
        scratch_shapes=[
            pltpu.VMEM((half, size, 2 * columns), f32),
            pltpu.VMEM((columns, blocks * size), f32),
            pltpu.VMEM((blocks, size, neighbours * size), f32),
            pltpu.VMEM((blocks, 2 * size, neighbours * size), jnp.bfloat16),
            pltpu.VMEM((slots * blocks, size, 2 * columns), jnp.bfloat16),
            pltpu.VMEM((slots, half, size, 2 * columns), f32),
            pltpu.VMEM((slots, half, size, 2 * columns), f32),
            pltpu.VMEM((groups, piece, 2 * columns), f32),
            pltpu.VMEM((groups, piece, 2 * columns), f32),
            pltpu.VMEM((piece, 2 * columns), f32),
            pltpu.VMEM((members, piece, 2 * columns), f32),
            pltpu.VMEM((piece, 2 * columns), f32),
            pltpu.VMEM((groups, piece, 2 * columns), f32),
            dma,
            dma((blocks,)),
            dma((2 * reach,)),
            dma((2 * reach,)),
            dma((2 * reach, half)),
            dma((2 * reach, half)),
            dma((6,)),
            pltpu.SemaphoreType.REGULAR((3,)),
            dma,
        ],
        compiler_params=pltpu.CompilerParams(
            collective_id=0, has_side_effects=True, vmem_limit_bytes=60 * 2**20
        ),
        name="filter",
    )(block_vectors.T, hamiltonian, pattern, owned_blocks, spectrum)
    total = float(blocks * size * groups * members) ** 0.5
    ortho, upper = pl.pallas_call(
        functools.partial(factor_kernel, total),
        out_shape=(
            jax.ShapeDtypeStruct((columns, blocks * size), f32),
            jax.ShapeDtypeStruct((columns, columns), f32),
        ),
        in_specs=[vmem, hbm],
        out_specs=(vmem, vmem),
        scratch_shapes=[pltpu.VMEM((half, size, 2 * columns), f32), dma],
        compiler_params=pltpu.CompilerParams(vmem_limit_bytes=60 * 2**20),
        name="factor",
    )(gram, filtered)
    return (ortho.T, upper)


def solution(mesh):
    placed = (
        P(("grp", "dev"), None),
        P(("grp", "dev"), None, None),
        P(("grp", "dev"), None),
        P(("grp", "dev")),
        P(),
    )
    return jax.shard_map(
        on_device,
        mesh=mesh,
        in_specs=placed,
        out_specs=(P(("grp", "dev"), None), P()),
        check_vma=False,
    )
```

time: 356 us -> 57.4 us (0.16)
  blocking collectives: 216 us -> 0 us
  Pallas kernels: 0 us -> 55.9 us
  local copies, waits for them, and re-layouts: 43.3 us -> 0 us
  other arithmetic: 32.9 us -> 0 us
  starting transfers between devices: 26.5 us -> 0 us
  matrix products: 21.5 us -> 0 us
  waiting for transfers between devices: 13.8 us -> 0 us
    psum x2 -> x0, blocking collectives: 216 us -> none  [summed_gram(): return lax.psum(local_gram, ('grp', 'dev'))]
    pallas_call x0 -> x2, Pallas kernels: none -> 55.9 us  [the longest x1 48.7 us: on_device(): pl.pallas_call(functools.partial(filter_kernel, groups, members, blocks,...]
    ppermute x8 -> x0, starting transfers between devices: 26.5 us -> none  [shifted(): return lax.ppermute(block, axis, route)]
    another operation x10 -> x0, other arithmetic: 24.3 us -> none  [the longest x6 13.1 us: cholesky_step(): upper = jnp.linalg.cholesky(gram_total).T]
    dot_general x5 -> x0, matrix products: 20.2 us -> none  [the longest x2 17.4 us: apply_matrix(): jnp.einsum('gik,gkc->gic', hamiltonian, picked, precision=lax.Precision.H...]
    reshape x4 -> x0, local copies, waits for them, and re-layouts: 16.8 us -> none  [the longest x2 15.6 us: apply_matrix(): picked.reshape(block_count, neighbours * values.shape[1], values.shape[2])]
    select_n x2 -> x0, local copies, waits for them, and re-layouts: 16 us -> none  [apply_matrix(): picked = jnp.take(extended, local_index, axis=0)]
    ppermute x8 -> x0, waiting for transfers between devices: 13.8 us -> none  [shifted(): return lax.ppermute(block, axis, route)]
  transfers between devices with their start and end apart: 8 -> 0, of which waited for: 3 -> 0; matrix products, arithmetic and copies ran while one was open for 1% -> 0% of each run, Pallas kernels for 0% -> 0%
where the time goes in v1:
time: 57.4 us; the launch traced here: 57.2 us
  Pallas kernels  55.9 us (97%)
  between operations  1.28 us (2%)
    pallas_call x1, Pallas kernels, on_device(): pl.pallas_call(functools.partial(filter_kernel, groups, members, blocks,...  48.7 us
    pallas_call x1, Pallas kernels, on_device(): pl.pallas_call(functools.partial(factor_kernel, total), out_shape=(jax.Sh...  7.22 us

profile of v1, /device:TPU:1, one launch (start us, length us, event | category | flops | bytes accessed | tf_op | source)
XLA Modules:
  0.0 57.2 jit_solution(10557234684982266693)
XLA Ops:
  1.3 48.7 %filter.1 = (f32[4,64,128]{2,1,0:T(8,128)}, f32[32,128]{1,0:T(8,128)}) custom-call(f32[64,512]{1,0:T(8,128)} %bitcast.2, f32[8,64,2048]{2,1,0:T(8,128)} %ham_ref.1, s32[8,32]{1,0:T(8,128)} %pat_ref.1, s32[1]{0:T(128)S(6)} %copy.7.owned_ref, f32[2]{0:T(128)} %spec_ref.1), custom_call_target="tpu_custom_call" | custom-call | tf_op jit(solution)/shard_map/filter/pallas_call | solution.py:328
  50.0 7.2 %factor.1 = (f32[64,512]{1,0:T(8,128)}, f32[64,64]{1,0:T(8,128)}) custom-call(f32[32,128]{1,0:T(8,128)} %get-tuple-element.6.g_ref, f32[4,64,128]{2,1,0:T(8,128)} %get-tuple-element.7.y_ref), custom_call_target="tpu_custom_call" | custom-call | tf_op jit(solution)/shard_map/factor/pallas_call | solution.py:366

commit v2 on v1

--- a/solution.py
+++ b/solution.py
@@ -21,13 +21,19 @@
     return pltpu.roll(value, value.shape[-1] // 2, value.ndim - 1)
 
 
+def halves(value):
+    high = value.astype(jnp.bfloat16)
+    return high, (value - high.astype(jnp.float32)).astype(jnp.bfloat16)
+
+
 def filter_kernel(
     groups, members, blocks, size, neighbours, reach,
-    xt_ref, ham_ref, pat_ref, owned_ref, spec_ref,
+    xt_ref, ham_ref, pat_in, owned_in, spec_in,
     y_out, g_out,
     y_buf, xt_buf, h_buf, h_split, v_split, ext_one, ext_two,
     part_buf, scatter_buf, own_buf, reduce_buf, sum_buf, total_buf,
-    xt_sem, h_sem, send_one, recv_one, send_two, recv_two, red_sem, round_sem, y_sem,
+    xt_sem, h_sem, sem_one, sem_two, red_sem, round_sem, y_sem,
+    pat_ref, owned_ref, spec_ref, small_sem,
 ):
     grp = lax.axis_index("grp")
     dev = lax.axis_index("dev")
@@ -46,15 +52,6 @@
     def in_members(step):
         return (grp, lax.rem(dev + step, members))
 
-    x_copy = pltpu.make_async_copy(xt_ref, xt_buf, xt_sem)
-    x_copy.start()
-
-    def h_copy(b):
-        return pltpu.make_async_copy(ham_ref.at[b], h_buf.at[b], h_sem.at[b])
-
-    for b in range(blocks):
-        h_copy(b).start()
-
     def distinct(offsets, count):
         return sorted({offset % count for offset in offsets} - {0})
 
@@ -63,8 +60,17 @@
             pl.semaphore_signal(sem, inc=1, device_id=target, device_id_type=MESH)
         return len(targets)
 
-    def group_ring(offsets):
-        return [in_groups(step) for step in distinct(offsets, groups)]
+    side = 4 if groups % 4 == 0 else groups
+    along_x, along_y = lax.div(grp, side), lax.rem(grp, side)
+
+    def plane(offsets_x, offsets_y):
+        return [
+            (lax.rem(along_x + step, groups // side) * side + along_y, dev)
+            for step in distinct(offsets_x, groups // side)
+        ] + [
+            (along_x * side + lax.rem(along_y + step, side), dev)
+            for step in distinct(offsets_y, side)
+        ]
 
     def member_ring(offsets):
         return [in_members(step) for step in distinct(offsets, members)]
@@ -76,14 +82,36 @@
     barrier = pltpu.get_barrier_semaphore()
     greeted = greet(
         barrier,
-        [peer(distance) for distance in distances]
-        + siblings
-        + member_ring((2, -2))
-        + group_ring((1, -1, 4, -4)),
-    )
+        siblings + member_ring((2, -2)) + plane((1, -1), (1, -1)),
+    )
+    for distance in distances:
+        inside = (flat + distance >= 0) & (flat + distance < devices)
+        greeted = greeted + jnp.where(inside, 1, 0)
+
+        @pl.when(inside)
+        def _():
+            greet(barrier, [peer(distance)])
+
+    small = [
+        pltpu.make_async_copy(source, target, small_sem.at[k])
+        for k, (source, target) in enumerate(
+            ((owned_in, owned_ref), (spec_in, spec_ref), (pat_in, pat_ref))
+        )
+    ]
+    for copy in small:
+        copy.start()
+    x_copy = pltpu.make_async_copy(xt_ref, xt_buf, xt_sem)
+    x_copy.start()
+
+    def h_copy(b):
+        return pltpu.make_async_copy(ham_ref.at[b], h_buf.at[b], h_sem.at[b])
+
+    for b in range(blocks):
+        h_copy(b).start()
+
     rounds = [
-        member_ring((2, -2)) + group_ring((1, -1, 4, -4)),
-        member_ring((4, -4)) + group_ring((4, -4)),
+        member_ring((2, -2)) + plane((1, -1), (1, -1)),
+        member_ring((4, -4)) + plane((2,), (2,)),
         member_ring((8, -8)),
     ]
 
@@ -94,6 +122,8 @@
         if rounds[k]:
             pl.semaphore_wait(round_sem.at[k], len(rounds[k]))
 
+    for copy in small:
+        copy.wait()
     owned = owned_ref[0]
     shift = spec_ref[0]
     scale = spec_ref[1]
@@ -115,31 +145,78 @@
         )
         ext_one[reach, p] = live(p) * both.T
 
-    def halo_one(k):
-        distance = distances[k]
+    core = lax.rem(dev, 2)
+    sibling = (grp, other_core)
+    far_slot, near_slot = 4 - 4 * core, 3 - 2 * core
+    early = peer(4 * core - 2)
+    late = peer(2 - 4 * core)
+    below = flat >= 2
+    above = flat < devices - 2
+    toward = jnp.where(core == 0, below, above)
+    away = jnp.where(core == 0, above, below)
+    sends = (toward, away, None, away)
+    receives = (away, toward, None, toward)
+
+    def given(condition, step):
+        if condition is None:
+            step()
+        else:
+            pl.when(condition)(step)
+
+    def halo(ext, sems, kind, p):
+        source, target, device = (
+            (reach, far_slot, early),
+            (reach, 4 * core, late),
+            (reach, 1 + 2 * core, sibling),
+            (far_slot, near_slot, sibling),
+        )[kind]
         return pltpu.make_async_remote_copy(
-            src_ref=ext_one.at[reach],
-            dst_ref=ext_one.at[reach - distance],
-            send_sem=send_one.at[k],
-            recv_sem=recv_one.at[k],
-            device_id=peer(distance),
+            src_ref=ext.at[source, p],
+            dst_ref=ext.at[target, p],
+            send_sem=sems.at[0, kind, p],
+            recv_sem=sems.at[1, kind, p],
+            device_id=device,
             device_id_type=MESH,
         )
 
-    def halo_two(k, p):
-        distance = distances[k]
-        return pltpu.make_async_remote_copy(
-            src_ref=ext_two.at[reach, p],
-            dst_ref=ext_two.at[reach - distance, p],
-            send_sem=send_two.at[k, p],
-            recv_sem=recv_two.at[k, p],
-            device_id=peer(distance),
-            device_id_type=MESH,
-        )
+    def send(ext, sems, kind, p):
+        given(sends[kind], lambda: halo(ext, sems, kind, p).start())
+
+    def arrive(ext, sems, kind):
+        def step():
+            for p in range(half):
+                halo(ext, sems, kind, p).wait_recv()
+
+        given(receives[kind], step)
+
+    def gather(ext, sems):
+        @pl.when(away)
+        def _():
+            for p in range(half):
+                halo(ext, sems, 0, p).wait_recv()
+                halo(ext, sems, 3, p).start()
+
+        arrive(ext, sems, 2)
+        split(ext, 3 - 2 * core)
+        split(ext, far_slot)
+        arrive(ext, sems, 1)
+        split(ext, 4 * core)
+        arrive(ext, sems, 3)
+        split(ext, 1 + 2 * core)
+
+    def drain(ext, sems):
+        for kind in range(4):
+
+            def step():
+                for p in range(half):
+                    halo(ext, sems, kind, p).wait_send()
+
+            given(sends[kind], step)
 
     pl.semaphore_wait(barrier, greeted)
-    for k in range(len(distances)):
-        halo_one(k).start()
+    for kind in range(3):
+        for p in range(half):
+            send(ext_one, sem_one, kind, p)
     greet_round(0)
 
     rows = 16
@@ -192,29 +269,22 @@
         return jnp.where(low, product(p), product(p + half))
 
     split(ext_one, reach)
-    for k in range(len(distances)):
-        halo_one(k).wait()
-        split(ext_one, reach - distances[k])
+    gather(ext_one, sem_one)
     end_round(0)
     greet_round(1)
 
-    @pl.loop(0, half)
-    def _(p):
+    for p in range(half):
         first = ext_one[reach, p]
         ext_two[reach, p] = live(p) * ((apply_matrix(p) - shift * first) / scale)
-        for k in range(len(distances)):
-            halo_two(k, p).start()
+        for kind in range(3):
+            send(ext_two, sem_two, kind, p)
 
     end_round(1)
     greet_round(2)
     split(ext_two, reach)
-    for k in range(len(distances)):
-        for p in range(half):
-            halo_two(k, p).wait()
-        split(ext_two, reach - distances[k])
-
-    @pl.loop(0, half)
-    def _(p):
+    gather(ext_two, sem_two)
+
+    for p in range(half):
         second = ext_two[reach, p]
         y_buf[p] = live(p) * (
             2.0 * (apply_matrix(p) - shift * second) / scale - ext_one[reach, p]
@@ -222,13 +292,14 @@
 
     y_copy = pltpu.make_async_copy(y_buf, y_out, y_sem)
     y_copy.start()
-    gram = jnp.zeros((LANES, LANES), jnp.float32)
-    for p in range(half):
-        value = y_buf[p]
-        gram += lax.dot_general(
-            value, value, (((0,), (0,)), ((), ())),
-            precision=HIGHEST, preferred_element_type=jnp.float32,
-        )
+    value = y_buf[...].reshape(half * size, LANES)
+    high, rest = halves(value)
+    high_t, rest_t = halves(value.T)
+    gram = jnp.dot(
+        high_t, jnp.concatenate([high, rest], axis=1), preferred_element_type=jnp.float32
+    )
+    gram = gram[:, :LANES] + gram[:, LANES:]
+    gram += jnp.dot(rest_t, high, preferred_element_type=jnp.float32)
     gram = gram[:size] + swap_halves(gram[size:])
     packed = jnp.where(
         low_lanes((size // 2, LANES)), gram[: size // 2], swap_halves(gram[size // 2 :])
@@ -275,7 +346,62 @@
     finish(total_buf, groups - 1, 2)
     for m in range(groups):
         g_out[m * piece : (m + 1) * piece, :] = total_buf[m]
+    drain(ext_one, sem_one)
+    drain(ext_two, sem_two)
     y_copy.wait()
+
+
+def eliminate(work):
+    rows, lanes = work.shape
+    tile = 8
+    count = rows // tile
+    blocks = [work[tile * r : tile * (r + 1)] for r in range(count)]
+    sub = lax.broadcasted_iota(jnp.int32, (tile, lanes), 0)
+
+    def spread(value):
+        return jnp.broadcast_to(value, (tile, lanes))
+
+    for q in range(count):
+        below = range(q, count)
+        column = [
+            {r: spread(blocks[r][:, tile * q + c : tile * q + c + 1]) for r in below}
+            for c in range(tile)
+        ]
+        lead = [spread(blocks[q][c : c + 1]) for c in range(tile)]
+        pivot = [[spread(column[d][q][c : c + 1]) for d in range(tile)] for c in range(tile)]
+        factors = []
+        scales = []
+        for c in range(0, tile, 2):
+            first, cross, second = pivot[c][c], pivot[c][c + 1], pivot[c + 1][c + 1]
+            inv_first = 1.0 / first
+            inv_second = first * (1.0 / (first * second - cross * cross))
+            scales += [inv_first, inv_second]
+            ratio = cross * inv_first
+            one = {r: column[c][r] * inv_first for r in below}
+            one[q] = jnp.where(sub > c, one[q], 0.0)
+            two = {r: (column[c + 1][r] - one[r] * cross) * inv_second for r in below}
+            two[q] = jnp.where(sub > c + 1, two[q], 0.0)
+            factors += [one, two]
+            lead[c + 1] = lead[c + 1] - ratio * lead[c]
+            rest = {e: pivot[c + 1][e] - ratio * pivot[c][e] for e in range(c + 2, tile)}
+            for d in range(c + 2, tile):
+                left = pivot[c][d] * inv_first
+                right = rest[d] * inv_second
+                for r in below:
+                    column[d][r] = column[d][r] - (one[r] * pivot[c][d] + two[r] * rest[d])
+                lead[d] = lead[d] - (left * lead[c] + right * lead[c + 1])
+                for e in range(d, tile):
+                    pivot[d][e] = pivot[d][e] - (left * pivot[c][e] + right * rest[e])
+        for r in below:
+            terms = [factors[c][r] * lead[c] for c in range(tile)]
+            while len(terms) > 1:
+                terms = [x + y for x, y in zip(terms[::2], terms[1::2])]
+            blocks[r] = blocks[r] - terms[0]
+        scale = scales[0]
+        for c in range(1, tile):
+            scale = jnp.where(sub == c, scales[c], scale)
+        blocks[q] = blocks[q] * jnp.sqrt(scale)
+    return jnp.concatenate(blocks, axis=0)
 
 
 def factor_kernel(total, g_ref, y_ref, q_out, r_out, y_buf, y_sem):
@@ -286,14 +412,9 @@
     work = jnp.concatenate([packed, swap_halves(packed)], axis=0)
     row = lax.broadcasted_iota(jnp.int32, (size, lanes), 0)
     col = lax.broadcasted_iota(jnp.int32, (size, lanes), 1)
-    work = jnp.where(col < size, work, jnp.where(col - size == row, 1.0, 0.0))
-    for j in range(size - 1):
-        lead = work[j : j + 1, :]
-        lead = lead * (1.0 / lead[:, j : j + 1])
-        factor = jnp.where(row > j, jnp.broadcast_to(work[:, j : j + 1], work.shape), 0.0)
-        work = work - factor * lead
-    diagonal = jnp.sum(jnp.where(row == col, work, 0.0), axis=1, keepdims=True)
-    work = work * (1.0 / jnp.sqrt(diagonal))
+    work = eliminate(
+        jnp.where(col < size, work, jnp.where(col - size == row, 1.0, 0.0))
+    )
     r_out[...] = jnp.where(col >= row, work, 0.0)[:, :size] * (1.0 / total)
     low = col < size
     inverse = jnp.concatenate(
@@ -301,13 +422,12 @@
     )
     inverse = inverse * total
     y_copy.wait()
-    for p in range(half):
-        ortho = lax.dot_general(
-            inverse, y_buf[p], (((1,), (1,)), ((), ())),
-            precision=HIGHEST, preferred_element_type=jnp.float32,
-        )
-        q_out[:, p * size : (p + 1) * size] = ortho[:size]
-        q_out[:, (p + half) * size : (p + half + 1) * size] = ortho[size:]
+    ortho = lax.dot_general(
+        inverse, y_buf[...].reshape(half * size, lanes), (((1,), (1,)), ((), ())),
+        precision=HIGHEST, preferred_element_type=jnp.float32,
+    )
+    q_out[:, : half * size] = ortho[:size]
+    q_out[:, half * size :] = ortho[size:]
 
 
 def on_device(block_vectors, hamiltonian, pattern, owned_blocks, spectrum):
@@ -322,7 +442,6 @@
     piece = size // 2 // groups
     f32 = jnp.float32
     vmem = pl.BlockSpec(memory_space=pltpu.VMEM)
-    smem = pl.BlockSpec(memory_space=pltpu.SMEM)
     hbm = pl.BlockSpec(memory_space=pltpu.HBM)
     dma = pltpu.SemaphoreType.DMA
     filtered, gram = pl.pallas_call(
@@ -331,7 +450,7 @@
             jax.ShapeDtypeStruct((half, size, 2 * columns), f32),
             jax.ShapeDtypeStruct((size // 2, 2 * columns), f32),
         ),
-        in_specs=[hbm, hbm, smem, smem, smem],
+        in_specs=[hbm] * 5,
         out_specs=(hbm, vmem),
         scratch_shapes=[
             pltpu.VMEM((half, size, 2 * columns), f32),
@@ -349,13 +468,15 @@
             pltpu.VMEM((groups, piece, 2 * columns), f32),
             dma,
             dma((blocks,)),
-            dma((2 * reach,)),
-            dma((2 * reach,)),
-            dma((2 * reach, half)),
-            dma((2 * reach, half)),
+            dma((2, 4, half)),
+            dma((2, 4, half)),
             dma((6,)),
             pltpu.SemaphoreType.REGULAR((3,)),
             dma,
+            pltpu.SMEM((blocks, neighbours), jnp.int32),
+            pltpu.SMEM((1,), jnp.int32),
+            pltpu.SMEM((2,), f32),
+            dma((3,)),
         ],
         compiler_params=pltpu.CompilerParams(
             collective_id=0, has_side_effects=True, vmem_limit_bytes=60 * 2**20

time: 57.4 us -> 51.8 us (0.902)
  Pallas kernels: 55.9 us -> 50.3 us
    pallas_call x1, Pallas kernels: 7.22 us -> 4.12 us  [on_device(): pl.pallas_call(functools.partial(factor_kernel, total), out_shape=(jax.Sh...]
    pallas_call x1, Pallas kernels: 48.7 us -> 46.2 us  [on_device(): pl.pallas_call(functools.partial(filter_kernel, groups, members, blocks,...]
where the time goes in v2:
time: 51.8 us; the launch traced here: 51.6 us
  Pallas kernels  50.3 us (97%)
  between operations  1.28 us (2%)
    pallas_call x1, Pallas kernels, on_device(): pl.pallas_call(functools.partial(filter_kernel, groups, members, blocks,...  46.2 us
    pallas_call x1, Pallas kernels, on_device(): pl.pallas_call(functools.partial(factor_kernel, total), out_shape=(jax.Sh...  4.12 us

profile of v2, /device:TPU:1, one launch (start us, length us, event | category | flops | bytes accessed | tf_op | source)
XLA Modules:
  0.0 51.6 jit_solution(7637934834049516010)
XLA Ops:
  1.3 46.2 %filter.1 = (f32[4,64,128]{2,1,0:T(8,128)}, f32[32,128]{1,0:T(8,128)}) custom-call(f32[64,512]{1,0:T(8,128)} %bitcast.2, f32[8,64,2048]{2,1,0:T(8,128)} %ham_ref.1, s32[8,32]{1,0:T(8,128)} %pat_in.1, s32[1]{0:T(128)S(6)} %copy.7.owned_in, f32[2]{0:T(128)} %spec_in.1), custom_call_target="tpu_custom_call" | custom-call | tf_op jit(solution)/shard_map/filter/pallas_call | solution.py:447
  47.5 4.1 %factor.1 = (f32[64,512]{1,0:T(8,128)}, f32[64,64]{1,0:T(8,128)}) custom-call(f32[32,128]{1,0:T(8,128)} %get-tuple-element.6.g_ref, f32[4,64,128]{2,1,0:T(8,128)} %get-tuple-element.7.y_ref), custom_call_target="tpu_custom_call" | custom-call | tf_op jit(solution)/shard_map/factor/pallas_call | solution.py:487

commit v3 on v2

--- a/solution.py
+++ b/solution.py
@@ -19,11 +19,6 @@
 
 def swap_halves(value):
     return pltpu.roll(value, value.shape[-1] // 2, value.ndim - 1)
-
-
-def halves(value):
-    high = value.astype(jnp.bfloat16)
-    return high, (value - high.astype(jnp.float32)).astype(jnp.bfloat16)
 
 
 def filter_kernel(
@@ -46,11 +41,19 @@
         other = lax.rem(flat + distance + devices, devices)
         return (lax.div(other, members), lax.rem(other, members))
 
-    def in_groups(step):
-        return (lax.rem(grp + step, groups), dev)
-
     def in_members(step):
         return (grp, lax.rem(dev + step, members))
+
+    x_copy = pltpu.make_async_copy(xt_ref, xt_buf, xt_sem)
+    x_copy.start()
+    small = [
+        pltpu.make_async_copy(source, target, small_sem.at[k])
+        for k, (source, target) in enumerate(
+            ((owned_in, owned_ref), (spec_in, spec_ref), (pat_in, pat_ref))
+        )
+    ]
+    for copy in small:
+        copy.start()
 
     def distinct(offsets, count):
         return sorted({offset % count for offset in offsets} - {0})
@@ -91,17 +94,6 @@
         @pl.when(inside)
         def _():
             greet(barrier, [peer(distance)])
-
-    small = [
-        pltpu.make_async_copy(source, target, small_sem.at[k])
-        for k, (source, target) in enumerate(
-            ((owned_in, owned_ref), (spec_in, spec_ref), (pat_in, pat_ref))
-        )
-    ]
-    for copy in small:
-        copy.start()
-    x_copy = pltpu.make_async_copy(xt_ref, xt_buf, xt_sem)
-    x_copy.start()
 
     def h_copy(b):
         return pltpu.make_async_copy(ham_ref.at[b], h_buf.at[b], h_sem.at[b])
@@ -214,7 +206,7 @@
             given(sends[kind], step)
 
     pl.semaphore_wait(barrier, greeted)
-    for kind in range(3):
+    for kind in (0, 2, 1):
         for p in range(half):
             send(ext_one, sem_one, kind, p)
     greet_round(0)
@@ -276,8 +268,10 @@
     for p in range(half):
         first = ext_one[reach, p]
         ext_two[reach, p] = live(p) * ((apply_matrix(p) - shift * first) / scale)
-        for kind in range(3):
+        for kind in (0, 2):
             send(ext_two, sem_two, kind, p)
+    for p in range(half):
+        send(ext_two, sem_two, 1, p)
 
     end_round(1)
     greet_round(2)
@@ -293,13 +287,10 @@
     y_copy = pltpu.make_async_copy(y_buf, y_out, y_sem)
     y_copy.start()
     value = y_buf[...].reshape(half * size, LANES)
-    high, rest = halves(value)
-    high_t, rest_t = halves(value.T)
-    gram = jnp.dot(
-        high_t, jnp.concatenate([high, rest], axis=1), preferred_element_type=jnp.float32
-    )
-    gram = gram[:, :LANES] + gram[:, LANES:]
-    gram += jnp.dot(rest_t, high, preferred_element_type=jnp.float32)
+    gram = lax.dot_general(
+        value, value, (((0,), (0,)), ((), ())),
+        precision=HIGHEST, preferred_element_type=jnp.float32,
+    )
     gram = gram[:size] + swap_halves(gram[size:])
     packed = jnp.where(
         low_lanes((size // 2, LANES)), gram[: size // 2], swap_halves(gram[size // 2 :])
@@ -309,10 +300,24 @@
         part_buf[m] = packed[m * piece : (m + 1) * piece]
     end_round(2)
 
-    def exchange(step, who, source, target, k):
+    def in_plane(step):
+        return (
+            lax.rem(along_x + step[0], groups // side) * side
+            + lax.rem(along_y + step[1], side),
+            dev,
+        )
+
+    def hops(step):
+        return sum(min(o, n - o) for o, n in zip(step, (groups // side, side)))
+
+    every = [(x, y) for x in range(groups // side) for y in range(side)]
+    far_groups = sorted(every, key=hops)[:0:-1]
+    far_members = sorted(range(1, members), key=lambda step: abs(2 * step - members))
+
+    def exchange(device, source, target, k):
         return pltpu.make_async_remote_copy(
             src_ref=source, dst_ref=target, send_sem=red_sem.at[2 * k],
-            recv_sem=red_sem.at[2 * k + 1], device_id=who(step), device_id_type=MESH,
+            recv_sem=red_sem.at[2 * k + 1], device_id=device, device_id_type=MESH,
         )
 
     def finish(buf, count, k):
@@ -321,26 +326,22 @@
                 buf.at[pl.ds(0, count)], buf.at[pl.ds(0, count)], red_sem.at[sem]
             ).wait()
 
-    @pl.loop(1, groups)
-    def _(step):
-        to = lax.rem(grp + step, groups)
-        exchange(step, in_groups, part_buf.at[to], scatter_buf.at[grp], 0).start()
+    for step in far_groups:
+        exchange(in_plane(step), part_buf.at[in_plane(step)[0]], scatter_buf.at[grp], 0).start()
 
     scatter_buf[grp] = part_buf[grp]
     finish(scatter_buf, groups - 1, 0)
     own_buf[...] = jnp.sum(scatter_buf[...], axis=0)
 
-    @pl.loop(1, members)
-    def _(step):
-        exchange(step, in_members, own_buf, reduce_buf.at[dev], 1).start()
+    for step in far_members:
+        exchange(in_members(step), own_buf, reduce_buf.at[dev], 1).start()
 
     reduce_buf[dev] = own_buf[...]
     finish(reduce_buf, members - 1, 1)
     sum_buf[...] = jnp.sum(reduce_buf[...], axis=0)
 
-    @pl.loop(1, groups)
-    def _(step):
-        exchange(step, in_groups, sum_buf, total_buf.at[grp], 2).start()
+    for step in far_groups:
+        exchange(in_plane(step), sum_buf, total_buf.at[grp], 2).start()
 
     total_buf[grp] = sum_buf[...]
     finish(total_buf, groups - 1, 2)

time: 51.8 us -> 50.4 us (0.973)
  Pallas kernels: 50.3 us -> 49 us
    pallas_call x1, Pallas kernels: 46.2 us -> 44.8 us  [on_device(): pl.pallas_call(functools.partial(filter_kernel, groups, members, blocks,...]
where the time goes in v3:
time: 50.4 us; the launch traced here: 50.2 us
  Pallas kernels  49 us (97%)
  between operations  1.28 us (3%)
    pallas_call x1, Pallas kernels, on_device(): pl.pallas_call(functools.partial(filter_kernel, groups, members, blocks,...  44.8 us
    pallas_call x1, Pallas kernels, on_device(): pl.pallas_call(functools.partial(factor_kernel, total), out_shape=(jax.Sh...  4.12 us

profile of v3, /device:TPU:1, one launch (start us, length us, event | category | flops | bytes accessed | tf_op | source)
XLA Modules:
  0.0 50.2 jit_solution(16669249155445347606)
XLA Ops:
  1.3 44.8 %filter.1 = (f32[4,64,128]{2,1,0:T(8,128)}, f32[32,128]{1,0:T(8,128)}) custom-call(f32[64,512]{1,0:T(8,128)} %bitcast.2, f32[8,64,2048]{2,1,0:T(8,128)} %ham_ref.1, s32[8,32]{1,0:T(8,128)} %pat_in.1, s32[1]{0:T(128)S(6)} %copy.7.owned_in, f32[2]{0:T(128)} %spec_in.1), custom_call_target="tpu_custom_call" | custom-call | tf_op jit(solution)/shard_map/filter/pallas_call | solution.py:448
  46.1 4.1 %factor.1 = (f32[64,512]{1,0:T(8,128)}, f32[64,64]{1,0:T(8,128)}) custom-call(f32[32,128]{1,0:T(8,128)} %get-tuple-element.6.g_ref, f32[4,64,128]{2,1,0:T(8,128)} %get-tuple-element.7.y_ref), custom_call_target="tpu_custom_call" | custom-call | tf_op jit(solution)/shard_map/factor/pallas_call | solution.py:488
